TPU v7x, 32 devices: a whole 2x2x4 slice. The times are simulated.
32 devices in a mesh: expert: 8 (over y, x, core), tensor: 4 (over z).
Axes of the slice: x: 2, y: 2, z: 4, core: 2. Of those that a mesh axis runs over, the one named last changes fastest.
Arguments:
- tokens: bfloat16 [256, 2560], P(('expert', 'tensor')), may hold values from -12 to 12
- expert_ids: int32 [256], P(('expert', 'tensor')), may hold values from 0 to 7, as said below
- slot_ids: int32 [256], P(('expert', 'tensor')), may hold values from 0 to 7
- router: bfloat16 [2560, 8], replicated, may hold values from -0.125 to 0.125
- w_gate: bfloat16 [8, 2560, 4096], P('expert', None, 'tensor'), may hold values from -0.125 to 0.125
- w_up: bfloat16 [8, 2560, 4096], P('expert', None, 'tensor'), may hold values from -0.125 to 0.125
- hidden_grad: bfloat16 [8, 64, 4096], P('expert', None, 'tensor'), may hold values from -6 to 6
Outputs:
- activation: bfloat16 [8, 64, 4096], P('expert', None, 'tensor')
- token_grad: bfloat16 [256, 2560], P(('expert', 'tensor'))
Inputs may be any that keep to these rules, and one draw needn't show every extreme that they name: expert_ids and slot_ids are drawn together. Within each aligned group of 32 consecutive tokens no two tokens share both expert and slot, so a group sends at most 8 tokens to one expert; in every draw one expert takes all 8 slots of every group.
All inputs are finite; a program needn't handle non-finite values.
Results may differ from a plain program's by a relative error of at most 0.02.
Values may be sent and summed in bfloat16 or wider, within the bound.
A program may use at most 64 MiB of HBM per device.

v0:
```python
import jax
import jax.numpy as jnp
from jax import lax
from jax.sharding import PartitionSpec as P


def route_slots(buffer):
    return lax.all_to_all(buffer, "expert", split_axis=0, concat_axis=0, tiled=True)


def shards(tokens, expert_ids, slot_ids, router, w_gate, w_up, hidden_grad):
    n_tensor = lax.axis_size("tensor")
    n_expert = lax.axis_size("expert")
    tok_rows, feature_width = tokens.shape
    experts_all = router.shape[1]
    rows_all = hidden_grad.shape[1]
    capacity = rows_all // n_expert
    piece_width = feature_width // n_tensor
    gate_weight = w_gate[0]
    up_weight = w_up[0]
    logits = jnp.dot(tokens, router, preferred_element_type=jnp.float32)
    picked_mask = expert_ids[:, None] == jnp.arange(experts_all, dtype=jnp.int32)[None, :]
    picked = jnp.sum(jnp.where(picked_mask, logits, 0.0), axis=1)
    router_score = jax.nn.sigmoid(picked)
    routed_in = (router_score[:, None] * tokens.astype(jnp.float32)).astype(jnp.bfloat16)
    routing = jnp.stack([expert_ids, slot_ids], axis=1)
    group_rows, group_routing = (
        lax.all_gather(routed_in, "tensor", axis=0, tiled=True),
        lax.all_gather(routing, "tensor", axis=0, tiled=True),
    )
    target_row = group_routing[:, 0] * capacity + group_routing[:, 1]
    outgoing = (
        jnp.zeros((experts_all * capacity, feature_width), jnp.bfloat16)
        .at[target_row]
        .set(group_rows)
    )
    arrived = lax.all_to_all(
        outgoing.reshape(experts_all, capacity, feature_width),
        "expert",
        split_axis=0,
        concat_axis=0,
        tiled=True,
    )
    arrived = arrived.reshape(rows_all, feature_width)
    gate_proj = jnp.dot(arrived, gate_weight, preferred_element_type=jnp.float32)
    lifted = jnp.dot(arrived, up_weight, preferred_element_type=jnp.float32)
    sigma_gate = jax.nn.sigmoid(gate_proj)
    silu_gate = gate_proj * sigma_gate
    silu_slope = sigma_gate * (1.0 + gate_proj * (1.0 - sigma_gate))
    activation = (silu_gate * lifted).astype(jnp.bfloat16)
    cotangent = hidden_grad[0].astype(jnp.float32)
    d_gate = (cotangent * lifted * silu_slope).astype(jnp.bfloat16)
    d_lifted = (cotangent * silu_gate).astype(jnp.bfloat16)
    contract = (((1,), (1,)), ((), ()))
    partial_value = lax.dot_general(
        d_gate, gate_weight, contract, preferred_element_type=jnp.float32
    )
    partial_value = partial_value + lax.dot_general(
        d_lifted, up_weight, contract, preferred_element_type=jnp.float32
    )
    summed = lax.psum_scatter(
        partial_value.astype(jnp.bfloat16), "tensor", scatter_dimension=1, tiled=True
    )
    returned = route_slots(summed.reshape(n_expert, capacity, piece_width)).reshape(
        experts_all * capacity, piece_width
    )
    mine_rows = returned[target_row]
    ordered = mine_rows.reshape(n_tensor, tok_rows, piece_width).transpose(1, 0, 2)
    returned_rows = lax.all_to_all(ordered, "tensor", split_axis=1, concat_axis=1, tiled=True)
    d_float = returned_rows.reshape(tok_rows, feature_width).astype(jnp.float32)
    inner = jnp.sum(tokens.astype(jnp.float32) * d_float, axis=1)
    router_column = lax.dot_general(
        picked_mask.astype(jnp.bfloat16), router, contract, preferred_element_type=jnp.float32
    )
    gradient = (
        router_score[:, None] * d_float
        + (inner * router_score * (1.0 - router_score))[:, None] * router_column
    )
    return (activation[None], gradient.astype(jnp.bfloat16))


def solution(mesh):
    in_specs = (
        P(("expert", "tensor"), None),
        P(("expert", "tensor")),
        P(("expert", "tensor")),
        P(),
        P("expert", None, "tensor"),
        P("expert", None, "tensor"),
        P("expert", None, "tensor"),
    )
    out_specs = (P("expert", None, "tensor"), P(("expert", "tensor"), None))
    return jax.shard_map(shards, mesh=mesh, in_specs=in_specs, out_specs=out_specs, check_vma=False)
```

profile of v0, /device:TPU:0, one launch (start us, length us, event | category | flops | bytes accessed | tf_op | source)
XLA Modules:
  0.0 105.8 jit_solution(10809232803567639701)
XLA Ops:
  7.2 0.0 copy-start
  7.2 0.0 copy-start.2
  7.2 0.0 reduce-scatter.4.cloned.1.call-start
  7.2 0.7 copy-done
  7.9 0.9 fusion.16
  8.9 0.9 fusion.31
  9.8 15.1 %all_gather.7 = bf16[32,2560]{1,0:T(8,128)(2,1)S(1)} all-gather(bf16[8,2560]{1,0:T(8,128)(2,1)S(1)} %fusion.31), channel_id=1, replica_groups=mesh['expert'=8,'tensor'=4] {'tensor'}, dimensions={0}, use_global_device_ids=true | all-gather | bytes 204800 | tf_op jit(solution)/shard_map/all_gather | solution.py:28
  24.9 0.7 add_bitcast_fusion
  25.6 11.4 %all-gather = s32[4,8,2]{1,2,0:T(2,128)S(1)} all-gather(s32[1,8,2]{1,2,0:T(2,128)S(1)} %add_bitcast_fusion), channel_id=1, replica_groups=mesh['expert'=8,'tensor'=4] {'tensor'}, dimensions={0}, use_global_device_ids=true | all-gather | bytes 320 | tf_op jit(solution)/shard_map/all_gather | solution.py:29
  36.9 0.1 reshape.62
  37.0 0.9 scatter_custom_fusion
  38.0 0.0 copy-start.1
  38.0 11.4 %all_to_all.15 = bf16[8,8,2560]{2,1,0:T(8,128)(2,1)S(1)} all-to-all(bf16[8,8,2560]{2,1,0:T(8,128)(2,1)S(1)} %bitcast.56), channel_id=1, replica_groups=mesh['expert'=8,'tensor'=4] {'expert'}, dimensions={0} | all-to-all | bytes 655360 | tf_op jit(solution)/shard_map/all_to_all | solution.py:37
  49.4 0.0 slice-start
  49.4 3.7 %fusion.6 = f32[64,1024]{1,0:T(8,128)S(1)} fusion(bf16[1,2560,1024]{2,1,0:T(8,128)(2,1)} %param.11, bf16[8,8,2560]{2,1,0:T(8,128)(2,1)S(1)} %all_to_all.15), kind=kOutput, calls=%fused_computation.8 | convolution fusion | flops 335544320 | bytes 5832704 | tf_op jit(solution)/shard_map/dot_general | solution.py:45
  53.1 0.0 copy-done.2
  53.1 0.0 copy-done.1
  53.1 0.0 slice-start.1
  53.1 1.7 %fusion = f32[64,2560]{1,0:T(8,128)S(1)} fusion(bf16[1,2560,1024]{2,1,0:T(8,128)(2,1)S(1)} %copy-done.1, bf16[1,64,1024]{2,1,0:T(8,128)(2,1)S(1)} %copy-done.2, f32[64,1024]{1,0:T(8,128)S(1)} %fusion.6), kind=kOutput, calls=%fused_computation.2 | convolution fusion | flops 336003072 | bytes 6291456 | tf_op jit(solution)/shard_map/dot_general | solution.py:58
  54.8 1.0 fusion.2
  55.8 0.0 slice-done
  55.9 0.0 slice-done.1
  55.9 0.0 copy-start.3
  55.9 0.0 copy-start.4
  55.9 1.7 %fusion.11 = bf16[64,2560]{1,0:T(8,128)(2,1)S(1)} fusion(f32[64,2560]{1,0:T(8,128)S(1)} %fusion, bf16[1,2560,1024]{2,1,0:T(8,128)(2,1)S(1)} %bitcast.53, f32[64,1024]{1,0:T(8,128)S(1)} %fusion.2, f32[64,1024]{1,0:T(8,128)S(1)} %fusion.6, bf16[1,64,1024]{2,1,0:T(8,128)(2,1)S(1)} %copy-done.2), kind=kOutput, calls=%fused_computation.11 | convolution fusion | flops 336592896 | bytes 6881280 | tf_op jit(solution)/shard_map/dot_general | solution.py:55
  57.6 1.1 %copy.11 = bf16[64,2560]{0,1:T(8,128)(2,1)} copy(bf16[64,2560]{1,0:T(8,128)(2,1)S(1)} %fusion.11) | data formatting | bytes 655360
  58.7 0.0 reduce-scatter.4.cloned.1.call-update
  58.7 18.7 %reduce-scatter.4.cloned.1.call-done = bf16[640,64]{1,0:T(8,128)(2,1)} async-done(((bf16[2560,64]{1,0:T(8,128)(2,1)}), bf16[640,64]{1,0:T(8,128)(2,1)}) %reduce-scatter.4.cloned.1.call-update) | async-done | bytes 81936
  77.4 1.7 %copy.12 = bf16[64,640]{1,0:T(8,128)(2,1)} copy(bf16[64,640]{0,1:T(8,128)(2,1)} %bitcast.59) | data formatting | bytes 163840
  79.1 3.7 %all-to-all-start.1 = ((bf16[8,8,640]{2,1,0:T(8,128)(2,1)}), bf16[8,8,640]{2,1,0:T(8,128)(2,1)S(1)}, u32[]{:S(2)}, u32[]{:S(2)}) async-start(bf16[8,8,640]{2,1,0:T(8,128)(2,1)} %bitcast.11), calls=%async_computation.1 | async-start | bytes 163840 | tf_op jit(solution)/shard_map/all_to_all | solution.py:8
  82.7 5.1 %all-to-all-done.1 = bf16[8,8,640]{2,1,0:T(8,128)(2,1)S(1)} async-done(((bf16[8,8,640]{2,1,0:T(8,128)(2,1)}), bf16[8,8,640]{2,1,0:T(8,128)(2,1)S(1)}, u32[]{:S(2)}, u32[]{:S(2)}) %all-to-all-start.1) | async-done | bytes 81952 | tf_op jit(solution)/shard_map/all_to_all | solution.py:8
  87.8 1.2 %gather_fusion = bf16[32,640]{1,0:T(8,128)(2,1)} fusion(bf16[64,640]{1,0:T(8,128)(2,1)S(1)} %bitcast.55, s32[1024]{0:T(1024)S(1)} %pad_clamp_fusion), kind=kCustom, calls=%fused_computation | custom fusion | bytes 82048 | tf_op jit(solution)/shard_map/gather | solution.py:67
  89.1 3.3 %all-to-all-start.2 = ((bf16[8,4,640]{2,0,1:T(8,128)(2,1)}), bf16[8,4,640]{2,0,1:T(8,128)(2,1)S(1)}, u32[]{:S(2)}, u32[]{:S(2)}) async-start(bf16[8,4,640]{2,0,1:T(8,128)(2,1)} %bitcast.14), calls=%async_computation.2 | async-start | bytes 81920 | tf_op jit(solution)/shard_map/all_to_all | solution.py:69
  92.4 0.7 fusion.25
  93.1 4.9 %all-to-all-done.2 = bf16[8,4,640]{2,0,1:T(8,128)(2,1)S(1)} async-done(((bf16[8,4,640]{2,0,1:T(8,128)(2,1)}), bf16[8,4,640]{2,0,1:T(8,128)(2,1)S(1)}, u32[]{:S(2)}, u32[]{:S(2)}) %all-to-all-start.2) | async-done | bytes 40992 | tf_op jit(solution)/shard_map/all_to_all | solution.py:69
  98.0 0.0 copy-done.3
  98.0 0.1 fusion.32
  98.2 0.0 copy-done.4
  98.2 0.8 fusion.15
  (6 shorter events, 0.0 us)
Async XLA Ops:
  7.2 0.8 copy-start
  7.2 45.9 %copy-start.2 = (bf16[1,64,1024]{2,1,0:T(8,128)(2,1)S(1)}, bf16[1,64,1024]{2,1,0:T(8,128)(2,1)}, u32[]{:S(2)}) copy-start(bf16[1,64,1024]{2,1,0:T(8,128)(2,1)} %param.13) | copy-start | bytes 393220
  7.2 70.2 %reduce-scatter.4.cloned.1.call-start = ((), (), s32[]{:S(2)}) async-start(), calls=%async_computation.4 | async-start | bytes 819200
  38.0 15.1 %copy-start.1 = (bf16[1,2560,1024]{2,1,0:T(8,128)(2,1)S(1)}, bf16[1,2560,1024]{2,1,0:T(8,128)(2,1)}, u32[]{:S(2)}) copy-start(bf16[1,2560,1024]{2,1,0:T(8,128)(2,1)} %param.12) | copy-start | bytes 15728644
  49.4 6.4 %slice-start = ((s8[5242880]{0:T(1024)(128)(4,1)}), s8[4194304]{0:T(1024)(128)(4,1)S(1)}, s32[]{:S(2)}) async-start(s8[5242880]{0:T(1024)(128)(4,1)} %bitcast.52), calls=%async_computation.5 | async-start | bytes 8388608
  53.1 2.8 %slice-start.1 = ((s8[5242880]{0:T(1024)(128)(4,1)}), s8[1048576]{0:T(1024)(128)(4,1)S(1)}, s32[]{:S(2)}) async-start(s8[5242880]{0:T(1024)(128)(4,1)} %bitcast.52), calls=%async_computation.6 | async-start | bytes 2097152
  55.9 42.1 %copy-start.3 = (bf16[8,2560]{1,0:T(8,128)(2,1)S(1)}, bf16[8,2560]{1,0:T(8,128)(2,1)}, u32[]{:S(2)}) copy-start(bf16[8,2560]{1,0:T(8,128)(2,1)} %param.7) | copy-start | bytes 122884
  55.9 42.3 %copy-start.4 = (s32[8]{0:T(128)S(1)}, s32[8]{0:T(128)}, u32[]{:S(2)}) copy-start(s32[8]{0:T(128)} %param.8) | copy-start | bytes 100
  79.1 8.8 %all-to-all-start.1 = ((bf16[8,8,640]{2,1,0:T(8,128)(2,1)}), bf16[8,8,640]{2,1,0:T(8,128)(2,1)S(1)}, u32[]{:S(2)}, u32[]{:S(2)}) async-start(bf16[8,8,640]{2,1,0:T(8,128)(2,1)} %bitcast.11), calls=%async_computation.1 | async-start | bytes 163840 | tf_op jit(solution)/shard_map/all_to_all | solution.py:8
  89.1 8.9 %all-to-all-start.2 = ((bf16[8,4,640]{2,0,1:T(8,128)(2,1)}), bf16[8,4,640]{2,0,1:T(8,128)(2,1)S(1)}, u32[]{:S(2)}, u32[]{:S(2)}) async-start(bf16[8,4,640]{2,0,1:T(8,128)(2,1)} %bitcast.14), calls=%async_computation.2 | async-start | bytes 81920 | tf_op jit(solution)/shard_map/all_to_all | solution.py:69
Sparse Core Ops, SparseCore 0:
  58.8 18.5 reduce-scatter.3
where the time goes:
time: 106 us
  blocking collectives  37.9 us (36%)
  waiting for transfers between devices  28.7 us (27%)
  between operations  14.2 us (13%)
  matrix products  9.85 us (9%)
  starting transfers between devices  6.96 us (7%)
  local copies, waits for them, and re-layouts  5.78 us (5%)
  other arithmetic  2.45 us (2%)
    unnamed x2, waiting for transfers between devices  18.7 us
    all_gather x1, blocking collectives, shards(): lax.all_gather(routed_in, 'tensor', axis=0, tiled=True)  15.1 us
    all_to_all x1, blocking collectives, shards(): lax.all_to_all(outgoing.reshape(experts_all, capacity, feature_width), 'e...  11.4 us
    all_gather x1, blocking collectives, shards(): lax.all_gather(routing, 'tensor', axis=0, tiled=True)  11.4 us
    all_to_all x1, waiting for transfers between devices, route_slots(): lax.all_to_all(buffer, 'expert', split_axis=0, concat_axis=0, tiled=True)  5.1 us
    all_to_all x1, waiting for transfers between devices, shards(): lax.all_to_all(ordered, 'tensor', split_axis=1, concat_axis=1, tiled=True)  4.91 us
    all_to_all x1, starting transfers between devices, route_slots(): lax.all_to_all(buffer, 'expert', split_axis=0, concat_axis=0, tiled=True)  3.65 us
    dot_general x1, matrix products, shards(): jnp.dot(arrived, gate_weight, preferred_element_type=jnp.float32)  3.65 us
  transfers between devices with their start and end apart: 3, of which 3 were waited for; matrix products, arithmetic and copies ran while one was open for 1% of the time, Pallas kernels for 0%

commit v1 on v0

v1 whole, which is shorter than its diff:
```python
import functools

import jax
import jax.numpy as jnp
from jax import lax
from jax.experimental import pallas as pl
from jax.experimental.pallas import tpu as pltpu
from jax.sharding import PartitionSpec as P

MESH = pl.DeviceIdType.MESH
F32 = jnp.float32
BF16 = jnp.bfloat16
LAG = 2


def each(count, body):
    if count <= 16:
        for index in range(count):
            body(index)
    else:

        def step(index, carry):
            body(index)
            return carry

        lax.fori_loop(0, count, step, 0)


def kernel(
    chunks,
    n_expert,
    n_tensor,
    tokens_hbm,
    expert_hbm,
    slot_hbm,
    router_hbm,
    gate_hbm,
    up_hbm,
    grad_hbm,
    act_hbm,
    out_hbm,
    tokens,
    expert_ids,
    slot_ids,
    router,
    w_gate,
    w_up,
    hidden_grad,
    act,
    out,
    ids,
    rows,
    sent,
    arrived,
    part,
    returned,
    mine,
    partials,
    acc_gate,
    acc_up,
    d_gate,
    d_lifted,
    d_rows,
    in_sem,
    w_sem,
    out_sem,
    ids_sem,
    rows_sem,
    slots_sem,
    part_sem,
    mine_sem,
):
    me_e = lax.axis_index("expert")
    me_t = lax.axis_index("tensor")
    tok_rows, width = tokens.shape
    piece = width // chunks
    capacity = arrived.shape[2]
    slots = n_expert * capacity
    group = n_tensor * tok_rows

    def span(c):
        return pl.ds(c * piece, piece)

    def peer_t(k):
        return lax.rem(me_t + k + 1, n_tensor)

    def peer_e(k):
        return lax.rem(me_e + k + 1, n_expert)

    def over_t(src, dst, sems, index, peer):
        return pltpu.make_async_remote_copy(
            src_ref=src,
            dst_ref=dst,
            send_sem=sems.at[(0, *index, peer)],
            recv_sem=sems.at[(1, *index, me_t)],
            device_id={"tensor": peer},
            device_id_type=MESH,
        )

    def over_e(src, dst, sems, index, peer):
        return pltpu.make_async_remote_copy(
            src_ref=src,
            dst_ref=dst,
            send_sem=sems.at[(0, *index, peer)],
            recv_sem=sems.at[(1, *index, me_e)],
            device_id={"expert": peer},
            device_id_type=MESH,
        )

    def landed(buffer, sems, index, peer, axis):
        pltpu.make_async_remote_copy(
            src_ref=buffer,
            dst_ref=buffer,
            send_sem=sems.at[(0, *index, peer)],
            recv_sem=sems.at[(1, *index, peer)],
            device_id={axis: peer},
            device_id_type=MESH,
        ).wait_recv()

    loads = [
        pltpu.make_async_copy(expert_hbm, expert_ids, in_sem.at[0]),
        pltpu.make_async_copy(slot_hbm, slot_ids, in_sem.at[1]),
        pltpu.make_async_copy(tokens_hbm, tokens, in_sem.at[2]),
        pltpu.make_async_copy(router_hbm, router, in_sem.at[3]),
        pltpu.make_async_copy(grad_hbm.at[0], hidden_grad, in_sem.at[4]),
    ]
    for load in loads[:4]:
        load.start()

    barrier = pltpu.get_barrier_semaphore()

    def greet_t(k):
        pl.semaphore_signal(
            barrier, inc=1, device_id={"tensor": peer_t(k)}, device_id_type=MESH
        )

    def greet_e(k):
        pl.semaphore_signal(
            barrier, inc=1, device_id={"expert": peer_e(k)}, device_id_type=MESH
        )

    each(n_tensor - 1, greet_t)
    each(n_expert - 1, greet_e)

    weight_loads = []
    for c in range(chunks):
        pair = (
            pltpu.make_async_copy(gate_hbm.at[0, span(c)], w_gate.at[span(c)], w_sem.at[0, c]),
            pltpu.make_async_copy(up_hbm.at[0, span(c)], w_up.at[span(c)], w_sem.at[1, c]),
        )
        weight_loads.append(pair)
        for load in pair:
            load.start()
    loads[4].start()

    loads[0].wait()
    loads[1].wait()
    row_index = lax.broadcasted_iota(jnp.int32, (tok_rows, 128), 0)
    expert_of = jnp.zeros((tok_rows, 128), jnp.int32)
    slot_of = jnp.zeros((tok_rows, 128), jnp.int32)
    for i in range(tok_rows):
        expert_of = jnp.where(row_index == i, expert_ids[i], expert_of)
        slot_of = jnp.where(row_index == i, slot_ids[i], slot_of)
    ids[me_t] = expert_of * capacity + slot_of
    picked = (
        expert_of[:, :1] == lax.broadcasted_iota(jnp.int32, (tok_rows, n_expert), 1)
    ).astype(F32)

    loads[2].wait()
    loads[3].wait()
    column = jnp.dot(picked.astype(BF16), router[...], preferred_element_type=F32)
    token_values = tokens[...].astype(F32)
    score = jax.nn.sigmoid(jnp.sum(token_values * column, axis=1, keepdims=True))
    routed = (score * token_values).astype(BF16)
    for c in range(chunks):
        rows[c, me_t] = routed[:, c * piece : (c + 1) * piece]

    pl.semaphore_wait(barrier, n_tensor + n_expert - 2)

    def send_ids(k):
        over_t(ids.at[me_t], ids.at[me_t], ids_sem, (), peer_t(k)).start()

    each(n_tensor - 1, send_ids)
    for c in range(chunks):

        def send_rows(k):
            over_t(rows.at[c, me_t], rows.at[c, me_t], rows_sem, (c,), peer_t(k)).start()

        each(n_tensor - 1, send_rows)

    each(n_tensor - 1, lambda k: landed(ids.at[peer_t(k)], ids_sem, (), peer_t(k), "tensor"))
    target = ids[...].reshape(group, 128)[:, :1]
    place = (target == lax.broadcasted_iota(jnp.int32, (group, slots), 1)).astype(F32).astype(BF16)

    def dispatch(c):
        each(
            n_tensor - 1,
            lambda k: landed(rows.at[c, peer_t(k)], rows_sem, (c,), peer_t(k), "tensor"),
        )
        group_rows = rows[c].astype(F32).reshape(group, piece).astype(BF16)
        placed = lax.dot_general(
            place, group_rows, (((0,), (0,)), ((), ())), preferred_element_type=F32
        )
        sent[c] = placed.reshape(n_expert, capacity, piece).astype(BF16)

        def send(k):
            peer = peer_e(k)
            over_e(sent.at[c, peer], arrived.at[c, me_e], slots_sem, (c,), peer).start()

        each(n_expert - 1, send)
        arrived[c, me_e] = sent[c, me_e]

    def project(c):
        each(
            n_expert - 1,
            lambda k: landed(arrived.at[c, peer_e(k)], slots_sem, (c,), peer_e(k), "expert"),
        )
        for load in weight_loads[c]:
            load.wait()
        lhs = arrived[c].astype(F32).reshape(slots, piece).astype(BF16)
        for total, weight in ((acc_gate, w_gate), (acc_up, w_up)):
            product = jnp.dot(lhs, weight[span(c)], preferred_element_type=F32)
            total[...] = product if c == 0 else total[...] + product

    for step in range(chunks + LAG):
        if step < chunks:
            dispatch(step)
        if step >= LAG:
            project(step - LAG)

    loads[4].wait()
    gate_proj = acc_gate[...]
    lifted = acc_up[...]
    cotangent = hidden_grad[...].astype(F32)
    sigma = jax.nn.sigmoid(gate_proj)
    silu = gate_proj * sigma
    slope = sigma * (1.0 + gate_proj * (1.0 - sigma))
    d_gate[...] = (cotangent * lifted * slope).astype(BF16)
    d_lifted[...] = (cotangent * silu).astype(BF16)
    act[...] = (silu * lifted).astype(BF16)
    store_act = pltpu.make_async_copy(act, act_hbm.at[0], out_sem.at[0])
    store_act.start()

    contract = (((1,), (1,)), ((), ()))

    def pull_back(c):
        value = lax.dot_general(
            d_gate[...], w_gate[span(c)], contract, preferred_element_type=F32
        ) + lax.dot_general(d_lifted[...], w_up[span(c)], contract, preferred_element_type=F32)
        part[c] = value.reshape(n_expert, capacity, piece).astype(BF16)

        def send(k):
            peer = peer_e(k)
            over_e(part.at[c, peer], returned.at[c, me_e], part_sem, (c,), peer).start()

        each(n_expert - 1, send)
        returned[c, me_e] = part[c, me_e]

    def collect(c):
        each(
            n_expert - 1,
            lambda k: landed(returned.at[c, peer_e(k)], part_sem, (c,), peer_e(k), "expert"),
        )
        slot_rows = returned[c].astype(F32).reshape(slots, piece).astype(BF16)
        token_rows = jnp.dot(place, slot_rows, preferred_element_type=F32)
        mine[c] = token_rows.reshape(n_tensor, tok_rows, piece).astype(BF16)

        def send(k):
            peer = peer_t(k)
            over_t(mine.at[c, peer], partials.at[c, me_t], mine_sem, (c,), peer).start()

        each(n_tensor - 1, send)
        partials[c, me_t] = mine[c, me_t]

    def add_up(c):
        each(
            n_tensor - 1,
            lambda k: landed(partials.at[c, peer_t(k)], mine_sem, (c,), peer_t(k), "tensor"),
        )
        summed = jnp.sum(partials[c].astype(F32), axis=0).astype(BF16).astype(F32)
        d_rows[:, span(c)] = summed
        return jnp.sum(
            token_values[:, c * piece : (c + 1) * piece] * summed, axis=1, keepdims=True
        )

    inner = jnp.zeros((tok_rows, 1), F32)
    for step in range(chunks + 2 * LAG):
        if step < chunks:
            pull_back(step)
        if LAG <= step < chunks + LAG:
            collect(step - LAG)
        if step >= 2 * LAG:
            inner = inner + add_up(step - 2 * LAG)

    gradient = score * d_rows[...] + (inner * score * (1.0 - score)) * column
    out[...] = gradient.astype(BF16)
    store_out = pltpu.make_async_copy(out, out_hbm, out_sem.at[1])
    store_out.start()

    def ids_gone(k):
        over_t(ids.at[me_t], ids.at[me_t], ids_sem, (), peer_t(k)).wait_send()

    each(n_tensor - 1, ids_gone)
    for c in range(chunks):

        def gone_t(k):
            peer = peer_t(k)
            over_t(rows.at[c, me_t], rows.at[c, me_t], rows_sem, (c,), peer).wait_send()
            over_t(mine.at[c, peer], partials.at[c, me_t], mine_sem, (c,), peer).wait_send()

        def gone_e(k):
            peer = peer_e(k)
            over_e(sent.at[c, peer], arrived.at[c, me_e], slots_sem, (c,), peer).wait_send()
            over_e(part.at[c, peer], returned.at[c, me_e], part_sem, (c,), peer).wait_send()

        each(n_tensor - 1, gone_t)
        each(n_expert - 1, gone_e)
    store_act.wait()
    store_out.wait()


def shards(tokens, expert_ids, slot_ids, router, w_gate, w_up, hidden_grad):
    n_tensor = lax.axis_size("tensor")
    n_expert = lax.axis_size("expert")
    tok_rows, width = tokens.shape
    slots, hidden = hidden_grad.shape[1:]
    capacity = slots // n_expert
    piece = max(p for p in range(128, 513, 128) if width % p == 0)
    chunks = width // piece
    by_expert = (chunks, n_expert, capacity, piece)
    by_tensor = (chunks, n_tensor, tok_rows, piece)
    dma = pltpu.SemaphoreType.DMA
    hbm = pl.BlockSpec(memory_space=pltpu.HBM)
    return pl.pallas_call(
        functools.partial(kernel, chunks, n_expert, n_tensor),
        out_shape=(
            jax.ShapeDtypeStruct(hidden_grad.shape, BF16),
            jax.ShapeDtypeStruct(tokens.shape, BF16),
        ),
        in_specs=[hbm] * 7,
        out_specs=(hbm, hbm),
        scratch_shapes=[
            pltpu.VMEM(tokens.shape, BF16),
            pltpu.SMEM(expert_ids.shape, jnp.int32),
            pltpu.SMEM(slot_ids.shape, jnp.int32),
            pltpu.VMEM(router.shape[::-1], BF16),
            pltpu.VMEM(w_gate.shape[1:], BF16),
            pltpu.VMEM(w_up.shape[1:], BF16),
            pltpu.VMEM((slots, hidden), BF16),
            pltpu.VMEM((slots, hidden), BF16),
            pltpu.VMEM(tokens.shape, BF16),
            pltpu.VMEM((n_tensor, tok_rows, 128), jnp.int32),
            pltpu.VMEM(by_tensor, BF16),
            pltpu.VMEM(by_expert, BF16),
            pltpu.VMEM(by_expert, BF16),
            pltpu.VMEM(by_expert, BF16),
            pltpu.VMEM(by_expert, BF16),
            pltpu.VMEM(by_tensor, BF16),
            pltpu.VMEM(by_tensor, BF16),
            pltpu.VMEM((slots, hidden), F32),
            pltpu.VMEM((slots, hidden), F32),
            pltpu.VMEM((slots, hidden), BF16),
            pltpu.VMEM((slots, hidden), BF16),
            pltpu.VMEM(tokens.shape, F32),
            dma((5,)),
            dma((2, chunks)),
            dma((2,)),
            dma((2, n_tensor)),
            dma((2, chunks, n_tensor)),
            dma((2, chunks, n_expert)),
            dma((2, chunks, n_expert)),
            dma((2, chunks, n_tensor)),
        ],
        compiler_params=pltpu.CompilerParams(
            collective_id=0, has_side_effects=True, vmem_limit_bytes=56 * 1024 * 1024
        ),
        name="routed_experts",
    )(tokens, expert_ids, slot_ids, router.T, w_gate, w_up, hidden_grad)


def solution(mesh):
    in_specs = (
        P(("expert", "tensor"), None),
        P(("expert", "tensor")),
        P(("expert", "tensor")),
        P(),
        P("expert", None, "tensor"),
        P("expert", None, "tensor"),
        P("expert", None, "tensor"),
    )
    out_specs = (P("expert", None, "tensor"), P(("expert", "tensor"), None))
    return jax.shard_map(shards, mesh=mesh, in_specs=in_specs, out_specs=out_specs, check_vma=False)
```

time: 106 us -> 37.3 us (0.35)
  blocking collectives: 37.9 us -> 0 us
  Pallas kernels: 0 us -> 33.5 us
  waiting for transfers between devices: 28.7 us -> 0 us
  between operations: 14.2 us -> 0.64 us
  matrix products: 9.85 us -> 0 us
  starting transfers between devices: 6.96 us -> 0 us
  local copies, waits for them, and re-layouts: 5.78 us -> 2.97 us
  other arithmetic: 2.45 us -> 0 us
    pallas_call x0 -> x1, Pallas kernels: none -> 33.5 us  [shards(): pl.pallas_call(functools.partial(kernel, chunks, n_expert, n_tensor), out...]
    all_gather x2 -> x0, blocking collectives: 26.5 us -> none  [the longest x1 15.1 us: shards(): lax.all_gather(routed_in, 'tensor', axis=0, tiled=True)]
    unnamed x2 -> x0, waiting for transfers between devices: 18.7 us -> none
    all_to_all x1 -> x0, blocking collectives: 11.4 us -> none  [shards(): lax.all_to_all(outgoing.reshape(experts_all, capacity, feature_width), 'e...]
    all_to_all x2 -> x0, waiting for transfers between devices: 10 us -> none  [the longest x1 5.1 us: route_slots(): lax.all_to_all(buffer, 'expert', split_axis=0, concat_axis=0, tiled=True)]
    dot_general x6 -> x0, matrix products: 9.85 us -> none  [the longest x1 3.65 us: shards(): jnp.dot(arrived, gate_weight, preferred_element_type=jnp.float32)]
    all_to_all x2 -> x0, starting transfers between devices: 6.92 us -> none  [the longest x1 3.65 us: route_slots(): lax.all_to_all(buffer, 'expert', split_axis=0, concat_axis=0, tiled=True)]
    gather x1 -> x0, local copies, waits for them, and re-layouts: 1.24 us -> none  [shards(): mine_rows = returned[target_row]]
  transfers between devices with their start and end apart: 3 -> 0, of which waited for: 3 -> 0; matrix products, arithmetic and copies ran while one was open for 1% -> 0% of each run, Pallas kernels for 0% -> 0%
where the time goes in v1:
time: 37.3 us; the launch traced here: 37.1 us
  Pallas kernels  33.5 us (90%)
  local copies, waits for them, and re-layouts  2.97 us (8%)
  between operations  0.64 us (2%)
    pallas_call x1, Pallas kernels, shards(): pl.pallas_call(functools.partial(kernel, chunks, n_expert, n_tensor), out...  33.5 us
    unnamed x2, local copies, waits for them, and re-layouts  2.97 us

profile of v1, /device:TPU:0, one launch (start us, length us, event | category | flops | bytes accessed | tf_op | source)
XLA Modules:
  0.0 37.1 jit_solution(16424079170549689684)
XLA Ops:
  0.6 33.5 %routed_experts.1 = (bf16[1,64,1024]{2,1,0:T(8,128)(2,1)}, bf16[8,2560]{1,0:T(8,128)(2,1)}) custom-call(bf16[8,2560]{1,0:T(8,128)(2,1)} %tokens_hbm.1, s32[8]{0:T(128)} %expert_hbm.1, s32[8]{0:T(128)} %slot_hbm.1, bf16[8,2560]{1,0:T(8,128)(2,1)} %bitcast.1, bf16[1,2560,1024]{2,1,0:T(8,128)(2,1)} %gate_hbm.1, bf16[1,2560,1024]{2,1,0:T(8,128)(2,1)} %up_hbm.1, ...), custom_call_target="tpu_custom_call" | custom-call | tf_op jit(solution)/shard_map/routed_experts/pallas_call | solution.py:334
  34.1 1.6 %copy.11 = bf16[1,64,1024]{2,1,0:T(8,128)(2,1)} copy(bf16[1,64,1024]{2,1,0:T(8,128)(2,1)} %get-tuple-element.4) | data formatting | bytes 262144
  35.7 1.4 %copy.12 = bf16[8,2560]{1,0:T(8,128)(2,1)} copy(bf16[8,2560]{1,0:T(8,128)(2,1)} %get-tuple-element.5) | data formatting | bytes 81920

commit v2 on v1

--- a/solution.py
+++ b/solution.py
@@ -37,8 +37,8 @@
     gate_hbm,
     up_hbm,
     grad_hbm,
-    act_hbm,
-    out_hbm,
+    act,
+    out,
     tokens,
     expert_ids,
     slot_ids,
@@ -46,8 +46,6 @@
     w_gate,
     w_up,
     hidden_grad,
-    act,
-    out,
     ids,
     rows,
     sent,
@@ -63,7 +61,6 @@
     d_rows,
     in_sem,
     w_sem,
-    out_sem,
     ids_sem,
     rows_sem,
     slots_sem,
@@ -91,8 +88,8 @@
         return pltpu.make_async_remote_copy(
             src_ref=src,
             dst_ref=dst,
-            send_sem=sems.at[(0, *index, peer)],
-            recv_sem=sems.at[(1, *index, me_t)],
+            send_sem=sems.at[0, index],
+            recv_sem=sems.at[1, index],
             device_id={"tensor": peer},
             device_id_type=MESH,
         )
@@ -101,21 +98,19 @@
         return pltpu.make_async_remote_copy(
             src_ref=src,
             dst_ref=dst,
-            send_sem=sems.at[(0, *index, peer)],
-            recv_sem=sems.at[(1, *index, me_e)],
+            send_sem=sems.at[0, index],
+            recv_sem=sems.at[1, index],
             device_id={"expert": peer},
             device_id_type=MESH,
         )
 
-    def landed(buffer, sems, index, peer, axis):
-        pltpu.make_async_remote_copy(
-            src_ref=buffer,
-            dst_ref=buffer,
-            send_sem=sems.at[(0, *index, peer)],
-            recv_sem=sems.at[(1, *index, peer)],
-            device_id={axis: peer},
-            device_id_type=MESH,
-        ).wait_recv()
+    def landed(buffer, sems, index, count):
+        whole = buffer.at[pl.ds(0, count)]
+        pltpu.make_async_copy(whole, whole, sems.at[1, index]).wait()
+
+    def left(buffer, sems, index, count):
+        whole = buffer.at[pl.ds(0, count)]
+        pltpu.make_async_copy(whole, whole, sems.at[0, index]).wait()
 
     loads = [
         pltpu.make_async_copy(expert_hbm, expert_ids, in_sem.at[0]),
@@ -178,25 +173,22 @@
     pl.semaphore_wait(barrier, n_tensor + n_expert - 2)
 
     def send_ids(k):
-        over_t(ids.at[me_t], ids.at[me_t], ids_sem, (), peer_t(k)).start()
+        over_t(ids.at[me_t], ids.at[me_t], ids_sem, 0, peer_t(k)).start()
 
     each(n_tensor - 1, send_ids)
     for c in range(chunks):
 
         def send_rows(k):
-            over_t(rows.at[c, me_t], rows.at[c, me_t], rows_sem, (c,), peer_t(k)).start()
+            over_t(rows.at[c, me_t], rows.at[c, me_t], rows_sem, c, peer_t(k)).start()
 
         each(n_tensor - 1, send_rows)
 
-    each(n_tensor - 1, lambda k: landed(ids.at[peer_t(k)], ids_sem, (), peer_t(k), "tensor"))
+    landed(ids, ids_sem, 0, n_tensor - 1)
     target = ids[...].reshape(group, 128)[:, :1]
     place = (target == lax.broadcasted_iota(jnp.int32, (group, slots), 1)).astype(F32).astype(BF16)
 
     def dispatch(c):
-        each(
-            n_tensor - 1,
-            lambda k: landed(rows.at[c, peer_t(k)], rows_sem, (c,), peer_t(k), "tensor"),
-        )
+        landed(rows.at[c], rows_sem, c, n_tensor - 1)
         group_rows = rows[c].astype(F32).reshape(group, piece).astype(BF16)
         placed = lax.dot_general(
             place, group_rows, (((0,), (0,)), ((), ())), preferred_element_type=F32
@@ -205,16 +197,13 @@
 
         def send(k):
             peer = peer_e(k)
-            over_e(sent.at[c, peer], arrived.at[c, me_e], slots_sem, (c,), peer).start()
+            over_e(sent.at[c, peer], arrived.at[c, me_e], slots_sem, c, peer).start()
 
         each(n_expert - 1, send)
         arrived[c, me_e] = sent[c, me_e]
 
     def project(c):
-        each(
-            n_expert - 1,
-            lambda k: landed(arrived.at[c, peer_e(k)], slots_sem, (c,), peer_e(k), "expert"),
-        )
+        landed(arrived.at[c], slots_sem, c, n_expert - 1)
         for load in weight_loads[c]:
             load.wait()
         lhs = arrived[c].astype(F32).reshape(slots, piece).astype(BF16)
@@ -237,9 +226,7 @@
     slope = sigma * (1.0 + gate_proj * (1.0 - sigma))
     d_gate[...] = (cotangent * lifted * slope).astype(BF16)
     d_lifted[...] = (cotangent * silu).astype(BF16)
-    act[...] = (silu * lifted).astype(BF16)
-    store_act = pltpu.make_async_copy(act, act_hbm.at[0], out_sem.at[0])
-    store_act.start()
+    act[0] = (silu * lifted).astype(BF16)
 
     contract = (((1,), (1,)), ((), ()))
 
@@ -251,32 +238,26 @@
 
         def send(k):
             peer = peer_e(k)
-            over_e(part.at[c, peer], returned.at[c, me_e], part_sem, (c,), peer).start()
+            over_e(part.at[c, peer], returned.at[c, me_e], part_sem, c, peer).start()
 
         each(n_expert - 1, send)
         returned[c, me_e] = part[c, me_e]
 
     def collect(c):
-        each(
-            n_expert - 1,
-            lambda k: landed(returned.at[c, peer_e(k)], part_sem, (c,), peer_e(k), "expert"),
-        )
+        landed(returned.at[c], part_sem, c, n_expert - 1)
         slot_rows = returned[c].astype(F32).reshape(slots, piece).astype(BF16)
         token_rows = jnp.dot(place, slot_rows, preferred_element_type=F32)
         mine[c] = token_rows.reshape(n_tensor, tok_rows, piece).astype(BF16)
 
         def send(k):
             peer = peer_t(k)
-            over_t(mine.at[c, peer], partials.at[c, me_t], mine_sem, (c,), peer).start()
+            over_t(mine.at[c, peer], partials.at[c, me_t], mine_sem, c, peer).start()
 
         each(n_tensor - 1, send)
         partials[c, me_t] = mine[c, me_t]
 
     def add_up(c):
-        each(
-            n_tensor - 1,
-            lambda k: landed(partials.at[c, peer_t(k)], mine_sem, (c,), peer_t(k), "tensor"),
-        )
+        landed(partials.at[c], mine_sem, c, n_tensor - 1)
         summed = jnp.sum(partials[c].astype(F32), axis=0).astype(BF16).astype(F32)
         d_rows[:, span(c)] = summed
         return jnp.sum(
@@ -294,29 +275,24 @@
 
     gradient = score * d_rows[...] + (inner * score * (1.0 - score)) * column
     out[...] = gradient.astype(BF16)
-    store_out = pltpu.make_async_copy(out, out_hbm, out_sem.at[1])
-    store_out.start()
-
-    def ids_gone(k):
-        over_t(ids.at[me_t], ids.at[me_t], ids_sem, (), peer_t(k)).wait_send()
-
-    each(n_tensor - 1, ids_gone)
+
+    left(ids, ids_sem, 0, n_tensor - 1)
     for c in range(chunks):
-
-        def gone_t(k):
-            peer = peer_t(k)
-            over_t(rows.at[c, me_t], rows.at[c, me_t], rows_sem, (c,), peer).wait_send()
-            over_t(mine.at[c, peer], partials.at[c, me_t], mine_sem, (c,), peer).wait_send()
-
-        def gone_e(k):
-            peer = peer_e(k)
-            over_e(sent.at[c, peer], arrived.at[c, me_e], slots_sem, (c,), peer).wait_send()
-            over_e(part.at[c, peer], returned.at[c, me_e], part_sem, (c,), peer).wait_send()
-
-        each(n_tensor - 1, gone_t)
-        each(n_expert - 1, gone_e)
-    store_act.wait()
-    store_out.wait()
+        left(rows.at[c], rows_sem, c, n_tensor - 1)
+        left(sent.at[c], slots_sem, c, n_expert - 1)
+        left(part.at[c], part_sem, c, n_expert - 1)
+        left(mine.at[c], mine_sem, c, n_tensor - 1)
+
+
+def finish(act_in, out_in, act_out, out_out, sem):
+    copies = (
+        pltpu.make_async_copy(act_in, act_out, sem.at[0]),
+        pltpu.make_async_copy(out_in, out_out, sem.at[1]),
+    )
+    for copy in copies:
+        copy.start()
+    for copy in copies:
+        copy.wait()
 
 
 def shards(tokens, expert_ids, slot_ids, router, w_gate, w_up, hidden_grad):
@@ -331,14 +307,16 @@
     by_tensor = (chunks, n_tensor, tok_rows, piece)
     dma = pltpu.SemaphoreType.DMA
     hbm = pl.BlockSpec(memory_space=pltpu.HBM)
-    return pl.pallas_call(
+    vmem = pl.BlockSpec(memory_space=pltpu.VMEM)
+    out_shape = (
+        jax.ShapeDtypeStruct(hidden_grad.shape, BF16),
+        jax.ShapeDtypeStruct(tokens.shape, BF16),
+    )
+    results = pl.pallas_call(
         functools.partial(kernel, chunks, n_expert, n_tensor),
-        out_shape=(
-            jax.ShapeDtypeStruct(hidden_grad.shape, BF16),
-            jax.ShapeDtypeStruct(tokens.shape, BF16),
-        ),
+        out_shape=(pltpu.VMEM(hidden_grad.shape, BF16), pltpu.VMEM(tokens.shape, BF16)),
         in_specs=[hbm] * 7,
-        out_specs=(hbm, hbm),
+        out_specs=(vmem, vmem),
         scratch_shapes=[
             pltpu.VMEM(tokens.shape, BF16),
             pltpu.SMEM(expert_ids.shape, jnp.int32),
@@ -347,8 +325,6 @@
             pltpu.VMEM(w_gate.shape[1:], BF16),
             pltpu.VMEM(w_up.shape[1:], BF16),
             pltpu.VMEM((slots, hidden), BF16),
-            pltpu.VMEM((slots, hidden), BF16),
-            pltpu.VMEM(tokens.shape, BF16),
             pltpu.VMEM((n_tensor, tok_rows, 128), jnp.int32),
             pltpu.VMEM(by_tensor, BF16),
             pltpu.VMEM(by_expert, BF16),
@@ -364,18 +340,25 @@
             pltpu.VMEM(tokens.shape, F32),
             dma((5,)),
             dma((2, chunks)),
-            dma((2,)),
-            dma((2, n_tensor)),
-            dma((2, chunks, n_tensor)),
-            dma((2, chunks, n_expert)),
-            dma((2, chunks, n_expert)),
-            dma((2, chunks, n_tensor)),
+            dma((2, 1)),
+            dma((2, chunks)),
+            dma((2, chunks)),
+            dma((2, chunks)),
+            dma((2, chunks)),
         ],
         compiler_params=pltpu.CompilerParams(
             collective_id=0, has_side_effects=True, vmem_limit_bytes=56 * 1024 * 1024
         ),
         name="routed_experts",
     )(tokens, expert_ids, slot_ids, router.T, w_gate, w_up, hidden_grad)
+    return pl.pallas_call(
+        finish,
+        out_shape=out_shape,
+        in_specs=[vmem] * 2,
+        out_specs=(hbm, hbm),
+        scratch_shapes=[dma((2,))],
+        name="move_results",
+    )(*results)
 
 
 def solution(mesh):

time: 37.3 us -> 34.7 us (0.930)
  local copies, waits for them, and re-layouts: 2.97 us -> 1.25 us
  Pallas kernels: 33.5 us -> 32.6 us
    pallas_call x1, Pallas kernels: 33.5 us -> 31 us  [shards(): pl.pallas_call(functools.partial(kernel, chunks, n_expert, n_tensor), out...]
    unnamed x2 -> x4, local copies, waits for them, and re-layouts: 2.97 us -> 1.25 us
    pallas_call x0 -> x1, Pallas kernels: none -> 1.58 us  [shards(): pl.pallas_call(finish, out_shape=out_shape, in_specs=[vmem] * 2, out_spec...]
where the time goes in v2:
time: 34.7 us; the launch traced here: 34.5 us
  Pallas kernels  32.6 us (94%)
  local copies, waits for them, and re-layouts  1.25 us (4%)
  between operations  0.65 us (2%)
    pallas_call x1, Pallas kernels, shards(): pl.pallas_call(functools.partial(kernel, chunks, n_expert, n_tensor), out...  31 us
    pallas_call x1, Pallas kernels, shards(): pl.pallas_call(finish, out_shape=out_shape, in_specs=[vmem] * 2, out_spec...  1.58 us
    unnamed x4, local copies, waits for them, and re-layouts  1.25 us

profile of v2, /device:TPU:0, one launch (start us, length us, event | category | flops | bytes accessed | tf_op | source)
XLA Modules:
  0.0 34.5 jit_solution(7675167143486931676)
XLA Ops:
  0.6 31.0 %routed_experts.1 = (bf16[1,64,1024]{2,1,0:T(8,128)(2,1)S(1)}, bf16[8,2560]{1,0:T(8,128)(2,1)S(1)}) custom-call(bf16[8,2560]{1,0:T(8,128)(2,1)} %tokens_hbm.1, s32[8]{0:T(128)} %expert_hbm.1, s32[8]{0:T(128)} %slot_hbm.1, bf16[8,2560]{1,0:T(8,128)(2,1)} %bitcast.1, bf16[1,2560,1024]{2,1,0:T(8,128)(2,1)} %gate_hbm.1, bf16[1,2560,1024]{2,1,0:T(8,128)(2,1)} %up_hbm.1, ...), custom_call_target="tpu_custom_call" | custom-call | tf_op jit(solution)/shard_map/routed_experts/pallas_call | solution.py:315
  31.7 0.0 copy-start
  31.7 0.6 %copy-done = bf16[1,64,1024]{2,1,0:T(8,128)(2,1)} copy-done((bf16[1,64,1024]{2,1,0:T(8,128)(2,1)}, bf16[1,64,1024]{2,1,0:T(8,128)(2,1)S(1)}, u32[]{:S(2)}) %copy-start) | copy-done | bytes 131096
  32.3 0.0 copy-start.1
  32.3 0.6 %copy-done.1 = bf16[8,2560]{1,0:T(8,128)(2,1)} copy-done((bf16[8,2560]{1,0:T(8,128)(2,1)}, bf16[8,2560]{1,0:T(8,128)(2,1)S(1)}, u32[]{:S(2)}) %copy-start.1) | copy-done | bytes 40984
  32.9 1.6 %move_results.1 = (bf16[1,64,1024]{2,1,0:T(8,128)(2,1)}, bf16[8,2560]{1,0:T(8,128)(2,1)}) custom-call(bf16[1,64,1024]{2,1,0:T(8,128)(2,1)} %copy-done, bf16[8,2560]{1,0:T(8,128)(2,1)} %copy-done.1), custom_call_target="tpu_custom_call" | custom-call | tf_op jit(solution)/shard_map/move_results/pallas_call | solution.py:354
Async XLA Ops:
  31.7 0.6 %copy-start = (bf16[1,64,1024]{2,1,0:T(8,128)(2,1)}, bf16[1,64,1024]{2,1,0:T(8,128)(2,1)S(1)}, u32[]{:S(2)}) copy-start(bf16[1,64,1024]{2,1,0:T(8,128)(2,1)S(1)} %get-tuple-element.4.act_in) | copy-start | bytes 393220
  32.3 0.6 %copy-start.1 = (bf16[8,2560]{1,0:T(8,128)(2,1)}, bf16[8,2560]{1,0:T(8,128)(2,1)S(1)}, u32[]{:S(2)}) copy-start(bf16[8,2560]{1,0:T(8,128)(2,1)S(1)} %get-tuple-element.5.out_in) | copy-start | bytes 122884

commit v3 on v2

--- a/solution.py
+++ b/solution.py
@@ -10,7 +10,7 @@
 MESH = pl.DeviceIdType.MESH
 F32 = jnp.float32
 BF16 = jnp.bfloat16
-LAG = 2
+LAG = 1
 
 
 def each(count, body):
@@ -185,14 +185,14 @@
 
     landed(ids, ids_sem, 0, n_tensor - 1)
     target = ids[...].reshape(group, 128)[:, :1]
-    place = (target == lax.broadcasted_iota(jnp.int32, (group, slots), 1)).astype(F32).astype(BF16)
+    place = (target == lax.broadcasted_iota(jnp.int32, (group, slots), 1)).astype(F32)
+    place_t = place.T.astype(BF16)
+    place = place.astype(BF16)
 
     def dispatch(c):
         landed(rows.at[c], rows_sem, c, n_tensor - 1)
         group_rows = rows[c].astype(F32).reshape(group, piece).astype(BF16)
-        placed = lax.dot_general(
-            place, group_rows, (((0,), (0,)), ((), ())), preferred_element_type=F32
-        )
+        placed = jnp.dot(place_t, group_rows, preferred_element_type=F32)
         sent[c] = placed.reshape(n_expert, capacity, piece).astype(BF16)
 
         def send(k):
@@ -284,35 +284,20 @@
         left(mine.at[c], mine_sem, c, n_tensor - 1)
 
 
-def finish(act_in, out_in, act_out, out_out, sem):
-    copies = (
-        pltpu.make_async_copy(act_in, act_out, sem.at[0]),
-        pltpu.make_async_copy(out_in, out_out, sem.at[1]),
-    )
-    for copy in copies:
-        copy.start()
-    for copy in copies:
-        copy.wait()
-
-
 def shards(tokens, expert_ids, slot_ids, router, w_gate, w_up, hidden_grad):
     n_tensor = lax.axis_size("tensor")
     n_expert = lax.axis_size("expert")
     tok_rows, width = tokens.shape
     slots, hidden = hidden_grad.shape[1:]
     capacity = slots // n_expert
-    piece = max(p for p in range(128, 513, 128) if width % p == 0)
+    piece = max(p for p in range(128, 1281, 128) if width % p == 0)
     chunks = width // piece
     by_expert = (chunks, n_expert, capacity, piece)
     by_tensor = (chunks, n_tensor, tok_rows, piece)
     dma = pltpu.SemaphoreType.DMA
     hbm = pl.BlockSpec(memory_space=pltpu.HBM)
     vmem = pl.BlockSpec(memory_space=pltpu.VMEM)
-    out_shape = (
-        jax.ShapeDtypeStruct(hidden_grad.shape, BF16),
-        jax.ShapeDtypeStruct(tokens.shape, BF16),
-    )
-    results = pl.pallas_call(
+    return pl.pallas_call(
         functools.partial(kernel, chunks, n_expert, n_tensor),
         out_shape=(pltpu.VMEM(hidden_grad.shape, BF16), pltpu.VMEM(tokens.shape, BF16)),
         in_specs=[hbm] * 7,
@@ -351,15 +336,6 @@
         ),
         name="routed_experts",
     )(tokens, expert_ids, slot_ids, router.T, w_gate, w_up, hidden_grad)
-    return pl.pallas_call(
-        finish,
-        out_shape=out_shape,
-        in_specs=[vmem] * 2,
-        out_specs=(hbm, hbm),
-        scratch_shapes=[dma((2,))],
-        name="move_results",
-    )(*results)
-
 
 def solution(mesh):
     in_specs = (

time: 34.7 us -> 30.1 us (0.87)
  Pallas kernels: 32.6 us -> 28.1 us
    pallas_call x1, Pallas kernels: 31 us -> 28.1 us  [shards(): pl.pallas_call(functools.partial(kernel, chunks, n_expert, n_tensor), out...]
    pallas_call x1 -> x0, Pallas kernels: 1.58 us -> none  [shards(): pl.pallas_call(finish, out_shape=out_shape, in_specs=[vmem] * 2, out_spec...]
    unnamed x4 -> x2, local copies, waits for them, and re-layouts: 1.25 us -> 1.27 us
where the time goes in v3:
time: 30.1 us; the launch traced here: 30 us
  Pallas kernels  28.1 us (93%)
  local copies, waits for them, and re-layouts  1.27 us (4%)
  between operations  0.64 us (2%)
    pallas_call x1, Pallas kernels, shards(): pl.pallas_call(functools.partial(kernel, chunks, n_expert, n_tensor), out...  28.1 us
    unnamed x2, local copies, waits for them, and re-layouts  1.27 us

profile of v3, /device:TPU:0, one launch (start us, length us, event | category | flops | bytes accessed | tf_op | source)
XLA Modules:
  0.0 30.0 jit_solution(3397441896222782029)
XLA Ops:
  0.6 28.1 %routed_experts.1 = (bf16[1,64,1024]{2,1,0:T(8,128)(2,1)S(1)}, bf16[8,2560]{1,0:T(8,128)(2,1)S(1)}) custom-call(bf16[8,2560]{1,0:T(8,128)(2,1)} %tokens_hbm.1, s32[8]{0:T(128)} %expert_hbm.1, s32[8]{0:T(128)} %slot_hbm.1, bf16[8,2560]{1,0:T(8,128)(2,1)} %bitcast.1, bf16[1,2560,1024]{2,1,0:T(8,128)(2,1)} %gate_hbm.1, bf16[1,2560,1024]{2,1,0:T(8,128)(2,1)} %up_hbm.1, ...), custom_call_target="tpu_custom_call" | custom-call | tf_op jit(solution)/shard_map/routed_experts/pallas_call | solution.py:300
  28.7 0.7 %copy.11 = bf16[1,64,1024]{2,1,0:T(8,128)(2,1)} copy(bf16[1,64,1024]{2,1,0:T(8,128)(2,1)S(1)} %get-tuple-element.2) | data formatting | bytes 262144
  29.4 0.6 %copy.12 = bf16[8,2560]{1,0:T(8,128)(2,1)} copy(bf16[8,2560]{1,0:T(8,128)(2,1)S(1)} %get-tuple-element.3) | data formatting | bytes 81920

commit v4 on v3

--- a/solution.py
+++ b/solution.py
@@ -10,7 +10,8 @@
 MESH = pl.DeviceIdType.MESH
 F32 = jnp.float32
 BF16 = jnp.bfloat16
-LAG = 1
+PARTS = 4
+UNIT = 256
 
 
 def each(count, body):
@@ -26,8 +27,14 @@
         lax.fori_loop(0, count, step, 0)
 
 
+def cut(width):
+    units = width // UNIT
+    bounds = [UNIT * ((2 * i * units + PARTS) // (2 * PARTS)) for i in range(PARTS)] + [width]
+    return [(low, high - low) for low, high in zip(bounds, bounds[1:]) if high > low]
+
+
 def kernel(
-    chunks,
+    spans,
     n_expert,
     n_tensor,
     tokens_hbm,
@@ -70,19 +77,27 @@
     me_e = lax.axis_index("expert")
     me_t = lax.axis_index("tensor")
     tok_rows, width = tokens.shape
-    piece = width // chunks
-    capacity = arrived.shape[2]
+    chunks = len(spans)
+    capacity = arrived.shape[1]
     slots = n_expert * capacity
     group = n_tensor * tok_rows
 
     def span(c):
-        return pl.ds(c * piece, piece)
+        return pl.ds(*spans[c])
+
+    def wrap(index, count):
+        return jnp.where(index >= count, index - count, index)
+
+    if n_tensor <= 16:
+        list_t = [wrap(me_t + k + 1, n_tensor) for k in range(n_tensor - 1)]
+    if n_expert <= 16:
+        list_e = [wrap(me_e + k + 1, n_expert) for k in range(n_expert - 1)]
 
     def peer_t(k):
-        return lax.rem(me_t + k + 1, n_tensor)
+        return list_t[k] if n_tensor <= 16 else wrap(me_t + k + 1, n_tensor)
 
     def peer_e(k):
-        return lax.rem(me_e + k + 1, n_expert)
+        return list_e[k] if n_expert <= 16 else wrap(me_e + k + 1, n_expert)
 
     def over_t(src, dst, sems, index, peer):
         return pltpu.make_async_remote_copy(
@@ -90,7 +105,7 @@
             dst_ref=dst,
             send_sem=sems.at[0, index],
             recv_sem=sems.at[1, index],
-            device_id={"tensor": peer},
+            device_id=(me_e, peer),
             device_id_type=MESH,
         )
 
@@ -100,17 +115,19 @@
             dst_ref=dst,
             send_sem=sems.at[0, index],
             recv_sem=sems.at[1, index],
-            device_id={"expert": peer},
+            device_id=(peer, me_t),
             device_id_type=MESH,
         )
 
-    def landed(buffer, sems, index, count):
-        whole = buffer.at[pl.ds(0, count)]
-        pltpu.make_async_copy(whole, whole, sems.at[1, index]).wait()
-
-    def left(buffer, sems, index, count):
-        whole = buffer.at[pl.ds(0, count)]
-        pltpu.make_async_copy(whole, whole, sems.at[0, index]).wait()
+    def await_all(sem, buffer, count, columns):
+        whole = buffer.at[pl.ds(0, count), :, columns]
+        pltpu.make_async_copy(whole, whole, sem).wait()
+
+    def landed(buffer, sems, c, count):
+        await_all(sems.at[1, c], buffer, count, span(c))
+
+    def left(buffer, sems, c, count):
+        await_all(sems.at[0, c], buffer, count, span(c))
 
     loads = [
         pltpu.make_async_copy(expert_hbm, expert_ids, in_sem.at[0]),
@@ -126,12 +143,12 @@
 
     def greet_t(k):
         pl.semaphore_signal(
-            barrier, inc=1, device_id={"tensor": peer_t(k)}, device_id_type=MESH
+            barrier, inc=1, device_id=(me_e, peer_t(k)), device_id_type=MESH
         )
 
     def greet_e(k):
         pl.semaphore_signal(
-            barrier, inc=1, device_id={"expert": peer_e(k)}, device_id_type=MESH
+            barrier, inc=1, device_id=(peer_e(k), me_t), device_id_type=MESH
         )
 
     each(n_tensor - 1, greet_t)
@@ -167,8 +184,7 @@
     token_values = tokens[...].astype(F32)
     score = jax.nn.sigmoid(jnp.sum(token_values * column, axis=1, keepdims=True))
     routed = (score * token_values).astype(BF16)
-    for c in range(chunks):
-        rows[c, me_t] = routed[:, c * piece : (c + 1) * piece]
+    rows[me_t] = routed
 
     pl.semaphore_wait(barrier, n_tensor + n_expert - 2)
 
@@ -178,44 +194,45 @@
     each(n_tensor - 1, send_ids)
     for c in range(chunks):
 
+        mine_rows = rows.at[me_t, :, span(c)]
+
         def send_rows(k):
-            over_t(rows.at[c, me_t], rows.at[c, me_t], rows_sem, c, peer_t(k)).start()
+            over_t(mine_rows, mine_rows, rows_sem, c, peer_t(k)).start()
 
         each(n_tensor - 1, send_rows)
 
-    landed(ids, ids_sem, 0, n_tensor - 1)
+    await_all(ids_sem.at[1, 0], ids, n_tensor - 1, pl.ds(0, 128))
     target = ids[...].reshape(group, 128)[:, :1]
     place = (target == lax.broadcasted_iota(jnp.int32, (group, slots), 1)).astype(F32)
     place_t = place.T.astype(BF16)
     place = place.astype(BF16)
 
     def dispatch(c):
-        landed(rows.at[c], rows_sem, c, n_tensor - 1)
-        group_rows = rows[c].astype(F32).reshape(group, piece).astype(BF16)
+        landed(rows, rows_sem, c, n_tensor - 1)
+        group_rows = rows[:, :, span(c)].astype(F32).reshape(group, spans[c][1]).astype(BF16)
         placed = jnp.dot(place_t, group_rows, preferred_element_type=F32)
-        sent[c] = placed.reshape(n_expert, capacity, piece).astype(BF16)
+        sent[:, :, span(c)] = placed.reshape(n_expert, capacity, spans[c][1]).astype(BF16)
 
         def send(k):
             peer = peer_e(k)
-            over_e(sent.at[c, peer], arrived.at[c, me_e], slots_sem, c, peer).start()
+            over_e(sent.at[peer, :, span(c)], arrived.at[me_e, :, span(c)], slots_sem, c, peer).start()
 
         each(n_expert - 1, send)
-        arrived[c, me_e] = sent[c, me_e]
+        arrived[me_e, :, span(c)] = sent[me_e, :, span(c)]
 
     def project(c):
-        landed(arrived.at[c], slots_sem, c, n_expert - 1)
+        landed(arrived, slots_sem, c, n_expert - 1)
         for load in weight_loads[c]:
             load.wait()
-        lhs = arrived[c].astype(F32).reshape(slots, piece).astype(BF16)
+        lhs = arrived[:, :, span(c)].astype(F32).reshape(slots, spans[c][1]).astype(BF16)
         for total, weight in ((acc_gate, w_gate), (acc_up, w_up)):
             product = jnp.dot(lhs, weight[span(c)], preferred_element_type=F32)
             total[...] = product if c == 0 else total[...] + product
 
-    for step in range(chunks + LAG):
-        if step < chunks:
-            dispatch(step)
-        if step >= LAG:
-            project(step - LAG)
+    for c in range(chunks):
+        dispatch(c)
+    for c in range(chunks):
+        project(c)
 
     loads[4].wait()
     gate_proj = acc_gate[...]
@@ -234,54 +251,51 @@
         value = lax.dot_general(
             d_gate[...], w_gate[span(c)], contract, preferred_element_type=F32
         ) + lax.dot_general(d_lifted[...], w_up[span(c)], contract, preferred_element_type=F32)
-        part[c] = value.reshape(n_expert, capacity, piece).astype(BF16)
+        part[:, :, span(c)] = value.reshape(n_expert, capacity, spans[c][1]).astype(BF16)
 
         def send(k):
             peer = peer_e(k)
-            over_e(part.at[c, peer], returned.at[c, me_e], part_sem, c, peer).start()
+            over_e(part.at[peer, :, span(c)], returned.at[me_e, :, span(c)], part_sem, c, peer).start()
 
         each(n_expert - 1, send)
-        returned[c, me_e] = part[c, me_e]
+        returned[me_e, :, span(c)] = part[me_e, :, span(c)]
 
     def collect(c):
-        landed(returned.at[c], part_sem, c, n_expert - 1)
-        slot_rows = returned[c].astype(F32).reshape(slots, piece).astype(BF16)
+        landed(returned, part_sem, c, n_expert - 1)
+        slot_rows = returned[:, :, span(c)].astype(F32).reshape(slots, spans[c][1]).astype(BF16)
         token_rows = jnp.dot(place, slot_rows, preferred_element_type=F32)
-        mine[c] = token_rows.reshape(n_tensor, tok_rows, piece).astype(BF16)
+        mine[:, :, span(c)] = token_rows.reshape(n_tensor, tok_rows, spans[c][1]).astype(BF16)
 
         def send(k):
             peer = peer_t(k)
-            over_t(mine.at[c, peer], partials.at[c, me_t], mine_sem, c, peer).start()
+            over_t(mine.at[peer, :, span(c)], partials.at[me_t, :, span(c)], mine_sem, c, peer).start()
 
         each(n_tensor - 1, send)
-        partials[c, me_t] = mine[c, me_t]
+        partials[me_t, :, span(c)] = mine[me_t, :, span(c)]
 
     def add_up(c):
-        landed(partials.at[c], mine_sem, c, n_tensor - 1)
-        summed = jnp.sum(partials[c].astype(F32), axis=0).astype(BF16).astype(F32)
+        landed(partials, mine_sem, c, n_tensor - 1)
+        summed = jnp.sum(partials[:, :, span(c)].astype(F32), axis=0).astype(BF16).astype(F32)
         d_rows[:, span(c)] = summed
-        return jnp.sum(
-            token_values[:, c * piece : (c + 1) * piece] * summed, axis=1, keepdims=True
-        )
+        return jnp.sum(tokens[:, span(c)].astype(F32) * summed, axis=1, keepdims=True)
 
     inner = jnp.zeros((tok_rows, 1), F32)
-    for step in range(chunks + 2 * LAG):
-        if step < chunks:
-            pull_back(step)
-        if LAG <= step < chunks + LAG:
-            collect(step - LAG)
-        if step >= 2 * LAG:
-            inner = inner + add_up(step - 2 * LAG)
+    for c in range(chunks):
+        pull_back(c)
+    for c in range(chunks):
+        collect(c)
+    for c in range(chunks):
+        inner = inner + add_up(c)
 
     gradient = score * d_rows[...] + (inner * score * (1.0 - score)) * column
     out[...] = gradient.astype(BF16)
 
-    left(ids, ids_sem, 0, n_tensor - 1)
-    for c in range(chunks):
-        left(rows.at[c], rows_sem, c, n_tensor - 1)
-        left(sent.at[c], slots_sem, c, n_expert - 1)
-        left(part.at[c], part_sem, c, n_expert - 1)
-        left(mine.at[c], mine_sem, c, n_tensor - 1)
+    await_all(ids_sem.at[0, 0], ids, n_tensor - 1, pl.ds(0, 128))
+    for c in range(chunks):
+        left(rows, rows_sem, c, n_tensor - 1)
+        left(sent, slots_sem, c, n_expert - 1)
+        left(part, part_sem, c, n_expert - 1)
+        left(mine, mine_sem, c, n_tensor - 1)
 
 
 def shards(tokens, expert_ids, slot_ids, router, w_gate, w_up, hidden_grad):
@@ -290,15 +304,15 @@
     tok_rows, width = tokens.shape
     slots, hidden = hidden_grad.shape[1:]
     capacity = slots // n_expert
-    piece = max(p for p in range(128, 1281, 128) if width % p == 0)
-    chunks = width // piece
-    by_expert = (chunks, n_expert, capacity, piece)
-    by_tensor = (chunks, n_tensor, tok_rows, piece)
+    spans = cut(width)
+    chunks = len(spans)
+    by_expert = (n_expert, capacity, width)
+    by_tensor = (n_tensor, tok_rows, width)
     dma = pltpu.SemaphoreType.DMA
     hbm = pl.BlockSpec(memory_space=pltpu.HBM)
     vmem = pl.BlockSpec(memory_space=pltpu.VMEM)
     return pl.pallas_call(
-        functools.partial(kernel, chunks, n_expert, n_tensor),
+        functools.partial(kernel, spans, n_expert, n_tensor),
         out_shape=(pltpu.VMEM(hidden_grad.shape, BF16), pltpu.VMEM(tokens.shape, BF16)),
         in_specs=[hbm] * 7,
         out_specs=(vmem, vmem),

time: 30.1 us -> 30.6 us (1.017)
  Pallas kernels: 28.1 us -> 28.6 us
    pallas_call x1, Pallas kernels: 28.1 us -> 28.6 us  [shards(): pl.pallas_call(functools.partial(kernel, spans, n_expert, n_tensor), out_...]
where the time goes in v4:
time: 30.6 us; the launch traced here: 30.5 us
  Pallas kernels  28.6 us (93%)
  local copies, waits for them, and re-layouts  1.27 us (4%)
  between operations  0.64 us (2%)
    pallas_call x1, Pallas kernels, shards(): pl.pallas_call(functools.partial(kernel, spans, n_expert, n_tensor), out_...  28.6 us
    unnamed x2, local copies, waits for them, and re-layouts  1.27 us

profile of v4, /device:TPU:0, one launch (start us, length us, event | category | flops | bytes accessed | tf_op | source)
XLA Modules:
  0.0 30.5 jit_solution(3093609334723872528)
XLA Ops:
  0.6 28.6 %routed_experts.1 = (bf16[1,64,1024]{2,1,0:T(8,128)(2,1)S(1)}, bf16[8,2560]{1,0:T(8,128)(2,1)S(1)}) custom-call(bf16[8,2560]{1,0:T(8,128)(2,1)} %tokens_hbm.1, s32[8]{0:T(128)} %expert_hbm.1, s32[8]{0:T(128)} %slot_hbm.1, bf16[8,2560]{1,0:T(8,128)(2,1)} %bitcast.1, bf16[1,2560,1024]{2,1,0:T(8,128)(2,1)} %gate_hbm.1, bf16[1,2560,1024]{2,1,0:T(8,128)(2,1)} %up_hbm.1, ...), custom_call_target="tpu_custom_call" | custom-call | tf_op jit(solution)/shard_map/routed_experts/pallas_call | solution.py:314
  29.2 0.7 %copy.11 = bf16[1,64,1024]{2,1,0:T(8,128)(2,1)} copy(bf16[1,64,1024]{2,1,0:T(8,128)(2,1)S(1)} %get-tuple-element.2) | data formatting | bytes 262144
  29.9 0.6 %copy.12 = bf16[8,2560]{1,0:T(8,128)(2,1)} copy(bf16[8,2560]{1,0:T(8,128)(2,1)S(1)} %get-tuple-element.3) | data formatting | bytes 81920

commit v5 on v4

--- a/solution.py
+++ b/solution.py
@@ -10,7 +10,7 @@
 MESH = pl.DeviceIdType.MESH
 F32 = jnp.float32
 BF16 = jnp.bfloat16
-PARTS = 4
+PARTS = 3
 UNIT = 256
 
 
@@ -161,9 +161,8 @@
             pltpu.make_async_copy(up_hbm.at[0, span(c)], w_up.at[span(c)], w_sem.at[1, c]),
         )
         weight_loads.append(pair)
-        for load in pair:
-            load.start()
-    loads[4].start()
+    for load in weight_loads[0]:
+        load.start()
 
     loads[0].wait()
     loads[1].wait()
@@ -201,6 +200,11 @@
 
         each(n_tensor - 1, send_rows)
 
+    for pair in weight_loads[1:]:
+        for load in pair:
+            load.start()
+    loads[4].start()
+
     await_all(ids_sem.at[1, 0], ids, n_tensor - 1, pl.ds(0, 128))
     target = ids[...].reshape(group, 128)[:, :1]
     place = (target == lax.broadcasted_iota(jnp.int32, (group, slots), 1)).astype(F32)
@@ -243,7 +247,6 @@
     slope = sigma * (1.0 + gate_proj * (1.0 - sigma))
     d_gate[...] = (cotangent * lifted * slope).astype(BF16)
     d_lifted[...] = (cotangent * silu).astype(BF16)
-    act[0] = (silu * lifted).astype(BF16)
 
     contract = (((1,), (1,)), ((), ()))
 
@@ -282,6 +285,8 @@
     inner = jnp.zeros((tok_rows, 1), F32)
     for c in range(chunks):
         pull_back(c)
+    gate_again = acc_gate[...]
+    act[0] = (gate_again * jax.nn.sigmoid(gate_again) * acc_up[...]).astype(BF16)
     for c in range(chunks):
         collect(c)
     for c in range(chunks):

time: 30.6 us -> 30 us (0.980)
  Pallas kernels: 28.6 us -> 27.9 us
    pallas_call x1, Pallas kernels: 28.6 us -> 27.9 us  [shards(): pl.pallas_call(functools.partial(kernel, spans, n_expert, n_tensor), out_...]
where the time goes in v5:
time: 30 us; the launch traced here: 29.9 us
  Pallas kernels  27.9 us (93%)
  local copies, waits for them, and re-layouts  1.27 us (4%)
  between operations  0.64 us (2%)
    pallas_call x1, Pallas kernels, shards(): pl.pallas_call(functools.partial(kernel, spans, n_expert, n_tensor), out_...  27.9 us
    unnamed x2, local copies, waits for them, and re-layouts  1.27 us

profile of v5, /device:TPU:0, one launch (start us, length us, event | category | flops | bytes accessed | tf_op | source)
XLA Modules:
  0.0 29.9 jit_solution(13609447981491993066)
XLA Ops:
  0.6 27.9 %routed_experts.1 = (bf16[1,64,1024]{2,1,0:T(8,128)(2,1)S(1)}, bf16[8,2560]{1,0:T(8,128)(2,1)S(1)}) custom-call(bf16[8,2560]{1,0:T(8,128)(2,1)} %tokens_hbm.1, s32[8]{0:T(128)} %expert_hbm.1, s32[8]{0:T(128)} %slot_hbm.1, bf16[8,2560]{1,0:T(8,128)(2,1)} %bitcast.1, bf16[1,2560,1024]{2,1,0:T(8,128)(2,1)} %gate_hbm.1, bf16[1,2560,1024]{2,1,0:T(8,128)(2,1)} %up_hbm.1, ...), custom_call_target="tpu_custom_call" | custom-call | tf_op jit(solution)/shard_map/routed_experts/pallas_call | solution.py:319
  28.6 0.7 %copy.11 = bf16[1,64,1024]{2,1,0:T(8,128)(2,1)} copy(bf16[1,64,1024]{2,1,0:T(8,128)(2,1)S(1)} %get-tuple-element.2) | data formatting | bytes 262144
  29.2 0.6 %copy.12 = bf16[8,2560]{1,0:T(8,128)(2,1)} copy(bf16[8,2560]{1,0:T(8,128)(2,1)S(1)} %get-tuple-element.3) | data formatting | bytes 81920

commit v6 on v5

--- a/solution.py
+++ b/solution.py
@@ -245,15 +245,13 @@
     sigma = jax.nn.sigmoid(gate_proj)
     silu = gate_proj * sigma
     slope = sigma * (1.0 + gate_proj * (1.0 - sigma))
-    d_gate[...] = (cotangent * lifted * slope).astype(BF16)
-    d_lifted[...] = (cotangent * silu).astype(BF16)
-
-    contract = (((1,), (1,)), ((), ()))
+    d_gate[...] = (cotangent * lifted * slope).T.astype(BF16)
+    d_lifted[...] = (cotangent * silu).T.astype(BF16)
 
     def pull_back(c):
-        value = lax.dot_general(
-            d_gate[...], w_gate[span(c)], contract, preferred_element_type=F32
-        ) + lax.dot_general(d_lifted[...], w_up[span(c)], contract, preferred_element_type=F32)
+        value = jnp.dot(w_gate[span(c)], d_gate[...], preferred_element_type=F32)
+        value = value + jnp.dot(w_up[span(c)], d_lifted[...], preferred_element_type=F32)
+        value = value.T
         part[:, :, span(c)] = value.reshape(n_expert, capacity, spans[c][1]).astype(BF16)
 
         def send(k):
@@ -339,8 +337,8 @@
             pltpu.VMEM(by_tensor, BF16),
             pltpu.VMEM((slots, hidden), F32),
             pltpu.VMEM((slots, hidden), F32),
-            pltpu.VMEM((slots, hidden), BF16),
-            pltpu.VMEM((slots, hidden), BF16),
+            pltpu.VMEM((hidden, slots), BF16),
+            pltpu.VMEM((hidden, slots), BF16),
             pltpu.VMEM(tokens.shape, F32),
             dma((5,)),
             dma((2, chunks)),

time: 30 us -> 30.8 us (1.027)
  Pallas kernels: 27.9 us -> 28.8 us
    pallas_call x1, Pallas kernels: 27.9 us -> 28.8 us  [shards(): pl.pallas_call(functools.partial(kernel, spans, n_expert, n_tensor), out_...]
where the time goes in v6:
time: 30.8 us; the launch traced here: 30.7 us
  Pallas kernels  28.8 us (94%)
  local copies, waits for them, and re-layouts  1.27 us (4%)
  between operations  0.64 us (2%)
    pallas_call x1, Pallas kernels, shards(): pl.pallas_call(functools.partial(kernel, spans, n_expert, n_tensor), out_...  28.8 us
    unnamed x2, local copies, waits for them, and re-layouts  1.27 us

profile of v6, /device:TPU:0, one launch (start us, length us, event | category | flops | bytes accessed | tf_op | source)
XLA Modules:
  0.0 30.7 jit_solution(12066004661052841812)
XLA Ops:
  0.6 28.8 %routed_experts.1 = (bf16[1,64,1024]{2,1,0:T(8,128)(2,1)S(1)}, bf16[8,2560]{1,0:T(8,128)(2,1)S(1)}) custom-call(bf16[8,2560]{1,0:T(8,128)(2,1)} %tokens_hbm.1, s32[8]{0:T(128)} %expert_hbm.1, s32[8]{0:T(128)} %slot_hbm.1, bf16[8,2560]{1,0:T(8,128)(2,1)} %bitcast.1, bf16[1,2560,1024]{2,1,0:T(8,128)(2,1)} %gate_hbm.1, bf16[1,2560,1024]{2,1,0:T(8,128)(2,1)} %up_hbm.1, ...), custom_call_target="tpu_custom_call" | custom-call | tf_op jit(solution)/shard_map/routed_experts/pallas_call | solution.py:317
  29.4 0.7 %copy.11 = bf16[1,64,1024]{2,1,0:T(8,128)(2,1)} copy(bf16[1,64,1024]{2,1,0:T(8,128)(2,1)S(1)} %get-tuple-element.2) | data formatting | bytes 262144
  30.1 0.6 %copy.12 = bf16[8,2560]{1,0:T(8,128)(2,1)} copy(bf16[8,2560]{1,0:T(8,128)(2,1)S(1)} %get-tuple-element.3) | data formatting | bytes 81920

commit v7 on v5

--- a/solution.py
+++ b/solution.py
@@ -46,7 +46,6 @@
     grad_hbm,
     act,
     out,
-    tokens,
     expert_ids,
     slot_ids,
     router,
@@ -54,6 +53,7 @@
     w_up,
     hidden_grad,
     ids,
+    scores,
     rows,
     sent,
     arrived,
@@ -69,6 +69,7 @@
     in_sem,
     w_sem,
     ids_sem,
+    scores_sem,
     rows_sem,
     slots_sem,
     part_sem,
@@ -76,7 +77,7 @@
 ):
     me_e = lax.axis_index("expert")
     me_t = lax.axis_index("tensor")
-    tok_rows, width = tokens.shape
+    tok_rows, width = out.shape
     chunks = len(spans)
     capacity = arrived.shape[1]
     slots = n_expert * capacity
@@ -132,7 +133,7 @@
     loads = [
         pltpu.make_async_copy(expert_hbm, expert_ids, in_sem.at[0]),
         pltpu.make_async_copy(slot_hbm, slot_ids, in_sem.at[1]),
-        pltpu.make_async_copy(tokens_hbm, tokens, in_sem.at[2]),
+        pltpu.make_async_copy(tokens_hbm, rows.at[me_t], in_sem.at[2]),
         pltpu.make_async_copy(router_hbm, router, in_sem.at[3]),
         pltpu.make_async_copy(grad_hbm.at[0], hidden_grad, in_sem.at[4]),
     ]
@@ -163,6 +164,17 @@
         weight_loads.append(pair)
     for load in weight_loads[0]:
         load.start()
+
+    def send_rows(c):
+        mine_rows = rows.at[me_t, :, span(c)]
+        each(
+            n_tensor - 1,
+            lambda k: over_t(mine_rows, mine_rows, rows_sem, c, peer_t(k)).start(),
+        )
+
+    loads[2].wait()
+    pl.semaphore_wait(barrier, n_tensor + n_expert - 2)
+    send_rows(0)
 
     loads[0].wait()
     loads[1].wait()
@@ -177,28 +189,19 @@
         expert_of[:, :1] == lax.broadcasted_iota(jnp.int32, (tok_rows, n_expert), 1)
     ).astype(F32)
 
-    loads[2].wait()
     loads[3].wait()
     column = jnp.dot(picked.astype(BF16), router[...], preferred_element_type=F32)
-    token_values = tokens[...].astype(F32)
+    token_values = rows[me_t].astype(F32)
     score = jax.nn.sigmoid(jnp.sum(token_values * column, axis=1, keepdims=True))
-    routed = (score * token_values).astype(BF16)
-    rows[me_t] = routed
-
-    pl.semaphore_wait(barrier, n_tensor + n_expert - 2)
+    scores[me_t] = jnp.broadcast_to(score, (tok_rows, 128))
 
     def send_ids(k):
         over_t(ids.at[me_t], ids.at[me_t], ids_sem, 0, peer_t(k)).start()
+        over_t(scores.at[me_t], scores.at[me_t], scores_sem, 0, peer_t(k)).start()
 
     each(n_tensor - 1, send_ids)
-    for c in range(chunks):
-
-        mine_rows = rows.at[me_t, :, span(c)]
-
-        def send_rows(k):
-            over_t(mine_rows, mine_rows, rows_sem, c, peer_t(k)).start()
-
-        each(n_tensor - 1, send_rows)
+    for c in range(1, chunks):
+        send_rows(c)
 
     for pair in weight_loads[1:]:
         for load in pair:
@@ -206,14 +209,17 @@
     loads[4].start()
 
     await_all(ids_sem.at[1, 0], ids, n_tensor - 1, pl.ds(0, 128))
+    await_all(scores_sem.at[1, 0], scores, n_tensor - 1, pl.ds(0, 128))
     target = ids[...].reshape(group, 128)[:, :1]
+    group_score = scores[...].reshape(group, 128)[:, :1]
     place = (target == lax.broadcasted_iota(jnp.int32, (group, slots), 1)).astype(F32)
     place_t = place.T.astype(BF16)
     place = place.astype(BF16)
 
     def dispatch(c):
         landed(rows, rows_sem, c, n_tensor - 1)
-        group_rows = rows[:, :, span(c)].astype(F32).reshape(group, spans[c][1]).astype(BF16)
+        raw_rows = rows[:, :, span(c)].astype(F32).reshape(group, spans[c][1])
+        group_rows = (group_score * raw_rows).astype(BF16)
         placed = jnp.dot(place_t, group_rows, preferred_element_type=F32)
         sent[:, :, span(c)] = placed.reshape(n_expert, capacity, spans[c][1]).astype(BF16)
 
@@ -280,7 +286,7 @@
         landed(partials, mine_sem, c, n_tensor - 1)
         summed = jnp.sum(partials[:, :, span(c)].astype(F32), axis=0).astype(BF16).astype(F32)
         d_rows[:, span(c)] = summed
-        return jnp.sum(tokens[:, span(c)].astype(F32) * summed, axis=1, keepdims=True)
+        return jnp.sum(rows[me_t, :, span(c)].astype(F32) * summed, axis=1, keepdims=True)
 
     inner = jnp.zeros((tok_rows, 1), F32)
     for c in range(chunks):
@@ -296,6 +302,7 @@
     out[...] = gradient.astype(BF16)
 
     await_all(ids_sem.at[0, 0], ids, n_tensor - 1, pl.ds(0, 128))
+    await_all(scores_sem.at[0, 0], scores, n_tensor - 1, pl.ds(0, 128))
     for c in range(chunks):
         left(rows, rows_sem, c, n_tensor - 1)
         left(sent, slots_sem, c, n_expert - 1)
@@ -322,7 +329,6 @@
         in_specs=[hbm] * 7,
         out_specs=(vmem, vmem),
         scratch_shapes=[
-            pltpu.VMEM(tokens.shape, BF16),
             pltpu.SMEM(expert_ids.shape, jnp.int32),
             pltpu.SMEM(slot_ids.shape, jnp.int32),
             pltpu.VMEM(router.shape[::-1], BF16),
@@ -330,6 +336,7 @@
             pltpu.VMEM(w_up.shape[1:], BF16),
             pltpu.VMEM((slots, hidden), BF16),
             pltpu.VMEM((n_tensor, tok_rows, 128), jnp.int32),
+            pltpu.VMEM((n_tensor, tok_rows, 128), F32),
             pltpu.VMEM(by_tensor, BF16),
             pltpu.VMEM(by_expert, BF16),
             pltpu.VMEM(by_expert, BF16),
@@ -345,6 +352,7 @@
             dma((5,)),
             dma((2, chunks)),
             dma((2, 1)),
+            dma((2, 1)),
             dma((2, chunks)),
             dma((2, chunks)),
             dma((2, chunks)),

time: 30 us -> 30.5 us (1.017)
  Pallas kernels: 27.9 us -> 28.4 us
    pallas_call x1, Pallas kernels: 27.9 us -> 28.4 us  [shards(): pl.pallas_call(functools.partial(kernel, spans, n_expert, n_tensor), out_...]
where the time goes in v7:
time: 30.5 us; the launch traced here: 30.3 us
  Pallas kernels  28.4 us (93%)
  local copies, waits for them, and re-layouts  1.27 us (4%)
  between operations  0.64 us (2%)
    pallas_call x1, Pallas kernels, shards(): pl.pallas_call(functools.partial(kernel, spans, n_expert, n_tensor), out_...  28.4 us
    unnamed x2, local copies, waits for them, and re-layouts  1.27 us

profile of v7, /device:TPU:0, one launch (start us, length us, event | category | flops | bytes accessed | tf_op | source)
XLA Modules:
  0.0 30.3 jit_solution(5234717310645724131)
XLA Ops:
  0.6 28.4 %routed_experts.1 = (bf16[1,64,1024]{2,1,0:T(8,128)(2,1)S(1)}, bf16[8,2560]{1,0:T(8,128)(2,1)S(1)}) custom-call(bf16[8,2560]{1,0:T(8,128)(2,1)} %tokens_hbm.1, s32[8]{0:T(128)} %expert_hbm.1, s32[8]{0:T(128)} %slot_hbm.1, bf16[8,2560]{1,0:T(8,128)(2,1)} %bitcast.1, bf16[1,2560,1024]{2,1,0:T(8,128)(2,1)} %gate_hbm.1, bf16[1,2560,1024]{2,1,0:T(8,128)(2,1)} %up_hbm.1, ...), custom_call_target="tpu_custom_call" | custom-call | tf_op jit(solution)/shard_map/routed_experts/pallas_call | solution.py:326
  29.1 0.7 %copy.11 = bf16[1,64,1024]{2,1,0:T(8,128)(2,1)} copy(bf16[1,64,1024]{2,1,0:T(8,128)(2,1)S(1)} %get-tuple-element.2) | data formatting | bytes 262144
  29.7 0.6 %copy.12 = bf16[8,2560]{1,0:T(8,128)(2,1)} copy(bf16[8,2560]{1,0:T(8,128)(2,1)S(1)} %get-tuple-element.3) | data formatting | bytes 81920

commit v8 on v5

--- a/solution.py
+++ b/solution.py
@@ -303,6 +303,17 @@
         left(mine, mine_sem, c, n_tensor - 1)
 
 
+def finish(act_in, out_in, act_out, out_out, sem):
+    copies = (
+        pltpu.make_async_copy(act_in, act_out, sem.at[0]),
+        pltpu.make_async_copy(out_in, out_out, sem.at[1]),
+    )
+    for copy in copies:
+        copy.start()
+    for copy in copies:
+        copy.wait()
+
+
 def shards(tokens, expert_ids, slot_ids, router, w_gate, w_up, hidden_grad):
     n_tensor = lax.axis_size("tensor")
     n_expert = lax.axis_size("expert")
@@ -316,7 +327,7 @@
     dma = pltpu.SemaphoreType.DMA
     hbm = pl.BlockSpec(memory_space=pltpu.HBM)
     vmem = pl.BlockSpec(memory_space=pltpu.VMEM)
-    return pl.pallas_call(
+    results = pl.pallas_call(
         functools.partial(kernel, spans, n_expert, n_tensor),
         out_shape=(pltpu.VMEM(hidden_grad.shape, BF16), pltpu.VMEM(tokens.shape, BF16)),
         in_specs=[hbm] * 7,
@@ -355,6 +366,18 @@
         ),
         name="routed_experts",
     )(tokens, expert_ids, slot_ids, router.T, w_gate, w_up, hidden_grad)
+    results = [pltpu.with_memory_space_constraint(value, pltpu.VMEM) for value in results]
+    return pl.pallas_call(
+        finish,
+        out_shape=(
+            jax.ShapeDtypeStruct(hidden_grad.shape, BF16),
+            jax.ShapeDtypeStruct(tokens.shape, BF16),
+        ),
+        in_specs=[vmem] * 2,
+        out_specs=(hbm, hbm),
+        scratch_shapes=[dma((2,))],
+        name="move_results",
+    )(*results)
 
 def solution(mesh):
     in_specs = (

time: 30 us -> 29.4 us (0.980)
  local copies, waits for them, and re-layouts: 1.27 us -> 0 us
  Pallas kernels: 27.9 us -> 28.6 us
    unnamed x2 -> x0, local copies, waits for them, and re-layouts: 1.27 us -> none
    pallas_call x0 -> x1, Pallas kernels: none -> 0.68 us  [shards(): pl.pallas_call(finish, out_shape=(jax.ShapeDtypeStruct(hidden_grad.shape,...]
where the time goes in v8:
time: 29.4 us; the launch traced here: 29.3 us
  Pallas kernels  28.6 us (97%)
  between operations  0.64 us (2%)
    pallas_call x1, Pallas kernels, shards(): pl.pallas_call(functools.partial(kernel, spans, n_expert, n_tensor), out_...  27.9 us
    pallas_call x1, Pallas kernels, shards(): pl.pallas_call(finish, out_shape=(jax.ShapeDtypeStruct(hidden_grad.shape,...  0.68 us

profile of v8, /device:TPU:0, one launch (start us, length us, event | category | flops | bytes accessed | tf_op | source)
XLA Modules:
  0.0 29.3 jit_solution(9328780557341076010)
XLA Ops:
  0.6 27.9 %routed_experts.1 = (bf16[1,64,1024]{2,1,0:T(8,128)(2,1)S(1)}, bf16[8,2560]{1,0:T(8,128)(2,1)S(1)}) custom-call(bf16[8,2560]{1,0:T(8,128)(2,1)} %tokens_hbm.1, s32[8]{0:T(128)} %expert_hbm.1, s32[8]{0:T(128)} %slot_hbm.1, bf16[8,2560]{1,0:T(8,128)(2,1)} %bitcast.1, bf16[1,2560,1024]{2,1,0:T(8,128)(2,1)} %gate_hbm.1, bf16[1,2560,1024]{2,1,0:T(8,128)(2,1)} %up_hbm.1, ...), custom_call_target="tpu_custom_call" | custom-call | tf_op jit(solution)/shard_map/routed_experts/pallas_call | solution.py:330
  28.6 0.7 %move_results.1 = (bf16[1,64,1024]{2,1,0:T(8,128)(2,1)}, bf16[8,2560]{1,0:T(8,128)(2,1)}) custom-call(bf16[1,64,1024]{2,1,0:T(8,128)(2,1)S(1)} %get-tuple-element.4.act_in, bf16[8,2560]{1,0:T(8,128)(2,1)S(1)} %get-tuple-element.5.out_in), custom_call_target="tpu_custom_call" | custom-call | tf_op jit(solution)/shard_map/move_results/pallas_call | solution.py:370
